TPU v7x, 128 devices: a whole 4x4x4 slice. The times are simulated.
128 devices in a mesh: tile: 16 (over z, y), seq: 8 (over x, core).
Axes of the slice: x: 4, y: 4, z: 4, core: 2. Of those that a mesh axis runs over, the one named last changes fastest.
Arguments:
- cls_tokens: bfloat16 [16384, 1536], P(('tile', 'seq')), may hold values from -6 to 6
- norm_gain: float32 [1536], replicated, may hold values from 0.5 to 1.5
- w_gate: bfloat16 [1536, 4096], P(None, 'tile'), may hold values from -0.15625 to 0.15625
- w_up: bfloat16 [1536, 4096], P(None, 'tile'), may hold values from -0.15625 to 0.15625
- w_down: bfloat16 [4096, 1536], P('tile'), may hold values from -0.09375 to 0.09375
- layer_scale: float32 [1536], replicated, may hold values from 0.25 to 1.75
- final_gain: float32 [1536], replicated, may hold values from 0.5 to 1.5
- w_embed: bfloat16 [1536, 768], replicated, may hold values from -0.15625 to 0.15625
- dest_pos: int32 [16384], P(('tile', 'seq')), may hold values from 0 to 16383, as said below
- tile_coords: int32 [2, 16384], P(None, ('tile', 'seq')), may hold values from 0 to 999
- attn_gain: float32 [768], replicated, may hold values from 0.5 to 1.5
- w_qkv: bfloat16 [768, 2304], replicated, may hold values from -4 to 4
- offsets: int32 [12], replicated, may hold values from 0 to 15
- w_out: bfloat16 [768, 768], replicated, may hold values from -0.21875 to 0.21875
Outputs:
- slide_out: bfloat16 [16384, 768], P(('tile', 'seq'))
Inputs may be any that keep to these rules, and one draw needn't show every extreme that they name: dest_pos holds each number of 0 to 16383 once; the 128 rows of one device go to the devices of the slide order in groups of 0, 1 or 2 rows a device, some pair carrying 2; every device receives 128 rows, 2 of them from the device 128 / 2 places before it in the slide order, counted round.
All inputs are finite; a program needn't handle non-finite values.
Results may differ from a plain program's by a relative error of at most 0.018.
Values may be sent and summed in bfloat16 or wider, within the bound.
No kernel may reach another device: no remote copies, remote signals or barrier semaphores. Data moves between devices by JAX's collectives and lax.ppermute only.
A program may use at most 128 MiB of HBM per device.

v0:
```python
import jax
import jax.numpy as jnp
from jax import lax
from jax.sharding import PartitionSpec as P

HEAD_COUNT = 12
HEAD_WIDTH = 64
SEGMENT_SPACING = 16


def layer_norm(sender_rows, gain):
    average = jnp.mean(sender_rows, axis=-1, keepdims=True)
    centered = sender_rows - average
    variance = jnp.mean(centered * centered, axis=-1, keepdims=True)
    return centered * lax.rsqrt(variance + 1e-06) * gain


def position_table(coords, hidden_width):
    quarter = hidden_width // 4
    frequency = 1.0 / 10000.0 ** (jnp.arange(quarter).astype(jnp.float32) / quarter)
    along_x = coords[:, 0:1].astype(jnp.float32) * frequency[None, :]
    along_y = coords[:, 1:2].astype(jnp.float32) * frequency[None, :]
    return jnp.concatenate(
        [jnp.sin(along_x), jnp.cos(along_x), jnp.sin(along_y), jnp.cos(along_y)], axis=1
    )


def attend(queries, key_rows, values):
    score_scale = queries.shape[-1] ** (-0.5)
    scores = (
        jnp.einsum("qhd,khd->hqk", queries, key_rows, preferred_element_type=jnp.float32)
        * score_scale
    )
    highest = jnp.max(scores, axis=-1, keepdims=True)
    weights = jnp.exp(scores - highest)
    totals = jnp.sum(weights, axis=-1, keepdims=True)
    mixed_rows = jnp.einsum(
        "hqk,khd->qhd", weights.astype(jnp.bfloat16), values, preferred_element_type=jnp.float32
    )
    result = mixed_rows / jnp.transpose(totals, (1, 0, 2))
    logsum = jnp.transpose((highest + jnp.log(totals))[:, :, 0])
    return (result, logsum)


def body(
    cls_tokens,
    norm_gain,
    w_gate,
    w_up,
    w_down,
    layer_scale,
    final_gain,
    w_embed,
    dest_pos,
    tile_coords,
    attn_gain,
    w_qkv,
    offsets,
    w_out,
):
    resident_rows = cls_tokens.shape[0]
    tokens = cls_tokens.astype(jnp.float32)
    normed = layer_norm(tokens, norm_gain).astype(jnp.bfloat16)
    shard_rows = lax.all_gather(normed, "tile", axis=0, tiled=True)
    gate_proj = jnp.dot(shard_rows, w_gate, preferred_element_type=jnp.float32)
    upward = jnp.dot(shard_rows, w_up, preferred_element_type=jnp.float32)
    hidden = (jax.nn.silu(gate_proj) * upward).astype(jnp.bfloat16)
    projected = lax.psum_scatter(
        jnp.dot(hidden, w_down, preferred_element_type=jnp.float32),
        "tile",
        scatter_dimension=0,
        tiled=True,
    )
    mixed_rows = tokens + layer_scale * projected
    final_rows = layer_norm(mixed_rows, final_gain).astype(jnp.bfloat16)
    embedded = jnp.dot(final_rows, w_embed, preferred_element_type=jnp.float32).astype(jnp.bfloat16)
    hidden_width = embedded.shape[1]
    tile_count = lax.axis_size("tile")
    seq_count = lax.axis_size("seq")
    devices = tile_count * seq_count
    capacity = 2 * max(1, resident_rows // devices)
    target = dest_pos // resident_rows
    row_ids = jnp.arange(resident_rows)
    earlier = (target[:, None] == target[None, :]) & (row_ids[None, :] < row_ids[:, None])
    slot_index = jnp.sum(earlier.astype(jnp.int32), axis=1)
    where_to = target * capacity + slot_index
    payload = jnp.zeros((devices * capacity, hidden_width), jnp.bfloat16).at[where_to].set(embedded)
    meta_rows = jnp.stack([dest_pos, tile_coords[0], tile_coords[1]], axis=1)
    meta_table = jnp.full((devices * capacity, 3), -1, jnp.int32).at[where_to].set(meta_rows)
    received, received_meta = (
        lax.all_to_all(
            payload.reshape(devices, capacity, hidden_width),
            ("tile", "seq"),
            split_axis=0,
            concat_axis=0,
            tiled=True,
        ),
        lax.all_to_all(
            meta_table.reshape(devices, capacity, 3),
            ("tile", "seq"),
            split_axis=0,
            concat_axis=0,
            tiled=True,
        ),
    )
    flat_rows = received.reshape(-1, hidden_width)
    flat_meta = received_meta.reshape(-1, 3)
    is_live = flat_meta[:, 0] >= 0
    local_slot = jnp.where(is_live, flat_meta[:, 0] % resident_rows, resident_rows)
    placed = (
        jnp.zeros((resident_rows, hidden_width), jnp.bfloat16)
        .at[local_slot]
        .set(flat_rows, mode="drop")
    )
    coords = (
        jnp.zeros((resident_rows, 2), jnp.int32).at[local_slot].set(flat_meta[:, 1:], mode="drop")
    )
    seq_in = placed.astype(jnp.float32) + position_table(coords, hidden_width)
    normed_seq = layer_norm(seq_in, attn_gain).astype(jnp.bfloat16)
    qkv = jnp.dot(normed_seq, w_qkv, preferred_element_type=jnp.float32).astype(jnp.bfloat16)
    queries = qkv[:, :hidden_width]
    keys_values = qkv[:, hidden_width:]
    segment_kv = lax.all_gather(keys_values, "seq", axis=0, tiled=True)
    near_out, nearby_logsumexp = attend(
        queries.reshape(resident_rows, HEAD_COUNT, HEAD_WIDTH),
        segment_kv[:, :hidden_width].reshape(-1, HEAD_COUNT, HEAD_WIDTH),
        segment_kv[:, hidden_width:].reshape(-1, HEAD_COUNT, HEAD_WIDTH),
    )
    kept_rows = jnp.arange(SEGMENT_SPACING, dtype=jnp.int32)[:, None] == offsets[None, :]

    def select(sender_rows, stacked_rows):
        head_grouped = sender_rows.reshape(
            resident_rows // SEGMENT_SPACING, SEGMENT_SPACING, stacked_rows, HEAD_COUNT, HEAD_WIDTH
        )
        sampled_rows = jnp.sum(
            jnp.where(
                kept_rows[None, :, None, :, None], head_grouped, jnp.zeros((), sender_rows.dtype)
            ),
            axis=1,
        )
        return sampled_rows.reshape(resident_rows // SEGMENT_SPACING, stacked_rows * hidden_width)

    far_kv = lax.all_gather(select(keys_values, 2), ("tile", "seq"), axis=0, tiled=True)
    far_out, far_lse = attend(
        select(queries, 1).reshape(-1, HEAD_COUNT, HEAD_WIDTH),
        far_kv[:, :hidden_width].reshape(-1, HEAD_COUNT, HEAD_WIDTH),
        far_kv[:, hidden_width:].reshape(-1, HEAD_COUNT, HEAD_WIDTH),
    )
    far_full = jnp.where(kept_rows[None, :, :, None], far_out[:, None], 0.0).reshape(
        resident_rows, HEAD_COUNT, HEAD_WIDTH
    )
    nearby_grouped = nearby_logsumexp.reshape(
        resident_rows // SEGMENT_SPACING, SEGMENT_SPACING, HEAD_COUNT
    )
    far_share = jnp.where(
        kept_rows[None], 1.0 / (1.0 + jnp.exp(nearby_grouped - far_lse[:, None])), 0.0
    ).reshape(resident_rows, HEAD_COUNT)
    combined = (1.0 - far_share)[:, :, None] * near_out + far_share[:, :, None] * far_full
    attn_rows = combined.reshape(resident_rows, hidden_width).astype(jnp.bfloat16)
    return (seq_in + jnp.dot(attn_rows, w_out, preferred_element_type=jnp.float32)).astype(
        jnp.bfloat16
    )


def solution(mesh):
    in_specs = (
        P(("tile", "seq"), None),
        P(),
        P(None, "tile"),
        P(None, "tile"),
        P("tile", None),
        P(),
        P(),
        P(),
        P(("tile", "seq")),
        P(None, ("tile", "seq")),
        P(),
        P(),
        P(),
        P(),
    )
    out_specs = P(("tile", "seq"), None)
    return jax.shard_map(body, mesh=mesh, in_specs=in_specs, out_specs=out_specs, check_vma=False)
```

profile of v0, /device:TPU:1, one launch (start us, length us, event | category | flops | bytes accessed | tf_op | source)
XLA Modules:
  0.0 357.2 jit_solution(11485548192163310712)
XLA Ops:
  6.5 1.3 convert_reduce_fusion
  7.8 1.2 fusion.31
  9.1 2.0 fusion.33
  11.2 64.7 %all-gather.4.cloned.1.call-done = bf16[2048,1536]{1,0:T(8,128)(2,1)} async-done(((bf16[128,1536]{1,0:T(8,128)(2,1)}), bf16[2048,1536]{1,0:T(8,128)(2,1)}) %all-gather.4.cloned.1.call-update) | async-done | bytes 6291472 | tf_op jit(solution)/shard_map/all_gather | solution.py:64
  75.9 6.1 %fusion.70 = f32[2048,256]{1,0:T(8,128)} fusion(bf16[2048,1536]{1,0:T(8,128)(2,1)} %all-gather.4.cloned.1.call-done, bf16[1536,256]{1,0:T(8,128)(2,1)} %param.16), kind=kOutput, calls=%fused_computation.112 | convolution fusion | flops 1610612736 | bytes 9175040 | tf_op jit(solution)/shard_map/dot_general | solution.py:65
  82.0 14.6 %fusion.7 = f32[2048,1536]{1,0:T(8,128)} fusion(bf16[256,1536]{1,0:T(8,128)(2,1)} %param.18, bf16[2048,1536]{1,0:T(8,128)(2,1)} %all-gather.4.cloned.1.call-done, bf16[1536,256]{1,0:T(8,128)(2,1)} %param.17, f32[2048,256]{1,0:T(8,128)} %fusion.70), kind=kOutput, calls=%fused_computation.14 | convolution fusion | flops 3224371200 | bytes 22544384 | tf_op jit(solution)/shard_map/dot_general | solution.py:69
  96.6 0.8 slice_bitcast_fusion.1
  97.4 1.2 pad_add_fusion
  98.6 1.4 copy.75
  100.0 0.7 and_select_fusion.1
  100.9 1.2 compare_select_fusion.4
  102.0 1.8 scatter_custom_fusion
  103.8 8.3 %all-to-all-start = ((s32[128,2,3]{2,1,0:T(2,128)}), s32[128,2,3]{2,1,0:T(2,128)}, u32[]{:S(2)}, u32[]{:S(2)}) async-start(s32[128,2,3]{2,1,0:T(2,128)} %bitcast.76), calls=%async_computation | async-start | bytes 262144 | tf_op jit(solution)/shard_map/all_to_all | solution.py:98
  112.8 9.2 %all-to-all-done = s32[128,2,3]{2,1,0:T(2,128)} async-done(((s32[128,2,3]{2,1,0:T(2,128)}), s32[128,2,3]{2,1,0:T(2,128)}, u32[]{:S(2)}, u32[]{:S(2)}) %all-to-all-start) | async-done | bytes 3104 | tf_op jit(solution)/shard_map/all_to_all | solution.py:98
  122.0 1.5 copy.93
  123.5 68.9 %reduce-scatter.2.cloned.1.call-done = f32[128,1536]{1,0:T(8,128)} async-done(((f32[2048,1536]{1,0:T(8,128)}), f32[128,1536]{1,0:T(8,128)}) %reduce-scatter.2.cloned.1.call-update) | async-done | bytes 786448 | tf_op jit(solution)/shard_map/reduce_scatter | solution.py:68
  192.4 1.5 fusion.39
  193.9 1.5 multiply_reduce_fusion.1
  195.4 2.9 convolution_convert_fusion.1
  198.3 2.3 scatter_custom_fusion.1
  200.6 1.9 reshape.194
  202.5 7.8 %all-to-all-start.1 = ((bf16[128,2,768]{2,1,0:T(2,128)(2,1)}), bf16[128,2,768]{2,1,0:T(2,128)(2,1)}, u32[]{:S(2)}, u32[]{:S(2)}) async-start(bf16[128,2,768]{2,1,0:T(2,128)(2,1)} %reshape.194), calls=%async_computation.2 | async-start | bytes 786432 | tf_op jit(solution)/shard_map/all_to_all | solution.py:91
  210.3 0.6 compare_select_fusion
  211.0 2.2 scatter_custom_fusion.3
  213.2 1.1 fusion.52
  214.3 2.5 multiply_sine_fusion.1
  216.7 5.6 %all-to-all-done.1 = bf16[128,2,768]{2,1,0:T(2,128)(2,1)} async-done(((bf16[128,2,768]{2,1,0:T(2,128)(2,1)}), bf16[128,2,768]{2,1,0:T(2,128)(2,1)}, u32[]{:S(2)}, u32[]{:S(2)}) %all-to-all-start.1) | async-done | bytes 393248 | tf_op jit(solution)/shard_map/all_to_all | solution.py:91
  222.3 1.9 reshape.224
  224.2 2.7 scatter_custom_fusion.2
  226.9 1.4 fusion.66
  228.6 0.7 convolution_convert_fusion
  229.3 0.8 copy-done.7
  230.1 0.8 slice.54
  231.0 2.6 reshape.199
  233.5 2.2 select_reduce_fusion
  235.8 1.6 reshape.200
  237.4 0.7 copy.80
  238.1 0.7 broadcast_in_dim.118
  238.7 0.7 broadcast_in_dim.119
  239.4 1.6 slice.53
  241.1 1.8 copy.81
  242.8 2.1 reshape.198
  244.9 1.9 select_reduce_fusion.1
  246.8 8.7 %all-gather.6.cloned.1.call-done = bf16[1024,1536]{1,0:T(8,128)(2,1)} async-done(((bf16[128,1536]{1,0:T(8,128)(2,1)}), bf16[1024,1536]{1,0:T(8,128)(2,1)}) %all-gather.6.cloned.1.call-update) | async-done | bytes 3145744 | tf_op jit(solution)/shard_map/all_gather | solution.py:123
  255.4 3.8 %fusion.68 = (bf16[1024,768]{1,0:T(8,128)(2,1)}, bf16[1024,768]{1,0:T(8,128)(2,1)}) fusion(bf16[1024,1536]{1,0:T(8,128)(2,1)} %all-gather.6.cloned.1.call-done), kind=kLoop, calls=%fused_computation.110 | loop fusion | bytes 6291456 | tf_op jit(solution)/shard_map/slice | solution.py:126
  259.2 2.6 copy.82
  261.9 2.6 copy.85
  264.5 2.6 multiply_reduce_fusion
  267.1 2.7 copy-done.1
  269.8 1.9 fusion.1
  271.7 52.7 %all-gather.8.cloned.1.call-done = bf16[1024,1536]{1,0:T(8,128)(2,1)} async-done(((bf16[8,1536]{1,0:T(8,128)(2,1)}), bf16[1024,1536]{1,0:T(8,128)(2,1)}) %all-gather.8.cloned.1.call-update) | async-done | bytes 3145744 | tf_op jit(solution)/shard_map/all_gather | solution.py:143
  324.3 3.8 %fusion.67 = (bf16[1024,768]{1,0:T(8,128)(2,1)}, bf16[1024,768]{1,0:T(8,128)(2,1)}) fusion(bf16[1024,1536]{1,0:T(8,128)(2,1)} %all-gather.8.cloned.1.call-done), kind=kLoop, calls=%fused_computation.109 | loop fusion | bytes 6291456 | tf_op jit(solution)/shard_map/slice | solution.py:146
  328.1 2.6 copy.83
  330.7 1.8 fusion.69
  332.5 0.7 copy-done.6
  334.1 0.7 sub.77
  334.8 1.5 sub.78
  336.2 2.6 copy.86
  338.8 2.1 fusion.15
  340.9 1.0 broadcast_in_dim.128
  341.9 2.1 copy.89
  344.0 0.7 broadcast_subtract_fusion
  344.8 4.8 %fusion.26 = bf16[128,12,64]{0,2,1:T(8,128)(2,1)S(1)} fusion(bf16[1024,12,64]{0,2,1:T(8,128)(2,1)} %bitcast.74, f32[12,128,1024]{2,1,0:T(8,128)} %copy-done.1, f32[12,128]{1,0:T(8,128)S(1)} %get-tuple-element.23, f32[128,12,64]{0,2,1:T(8,128)} %copy.89, f32[128,12]{0,1:T(8,128)S(1)} %get-tuple-element.8, f32[128,12]{0,1:T(8,128)} %bitcast.79, ...), kind=kOutput, calls=%fused_computation.33 | convolution fusion | flops 206635008 | bytes 8480256 | tf_op jit(solution)/shard_map/hqk,khd->qhd/dot_general | solution.py:37
  349.6 1.0 fusion.14
  (45 shorter events, 2.0 us)
Async XLA Ops:
  6.5 222.0 %copy-start = (bf16[768,2304]{1,0:T(8,128)(2,1)S(1)}, bf16[768,2304]{1,0:T(8,128)(2,1)}, u32[]{:S(2)}) copy-start(bf16[768,2304]{1,0:T(8,128)(2,1)} %param.25) | copy-start | bytes 10616836
  6.5 69.4 %all-gather.4.cloned.1.call-start = ((), (), s32[]{:S(2)}) async-start(), calls=%async_computation.3 | async-start | bytes 6684672 | tf_op jit(solution)/shard_map/all_gather | solution.py:64
  11.1 181.2 %reduce-scatter.2.cloned.1.call-start = ((), (), s32[]{:S(2)}) async-start(), calls=%async_computation.4 | async-start | bytes 13369344 | tf_op jit(solution)/shard_map/reduce_scatter | solution.py:68
  96.6 95.8 %copy-start.9 = (f32[1536]{0:T(1024)S(1)}, f32[1536]{0:T(1024)}, u32[]{:S(2)}) copy-start(f32[1536]{0:T(1024)} %param.19) | copy-start | bytes 18436
  96.6 98.8 %copy-start.11 = (f32[1536]{0:T(1024)S(1)}, f32[1536]{0:T(1024)}, u32[]{:S(2)}) copy-start(f32[1536]{0:T(1024)} %param.20) | copy-start | bytes 18436
  103.8 18.1 %all-to-all-start = ((s32[128,2,3]{2,1,0:T(2,128)}), s32[128,2,3]{2,1,0:T(2,128)}, u32[]{:S(2)}, u32[]{:S(2)}) async-start(s32[128,2,3]{2,1,0:T(2,128)} %bitcast.76), calls=%async_computation | async-start | bytes 262144 | tf_op jit(solution)/shard_map/all_to_all | solution.py:98
  192.4 3.0 copy-start.2
  192.4 3.0 copy-start.3
  200.6 28.0 %copy-start.12 = (f32[768]{0:T(1024)S(1)}, f32[768]{0:T(1024)}, u32[]{:S(2)}) copy-start(f32[768]{0:T(1024)} %param.24) | copy-start | bytes 9220
  202.5 19.8 %all-to-all-start.1 = ((bf16[128,2,768]{2,1,0:T(2,128)(2,1)}), bf16[128,2,768]{2,1,0:T(2,128)(2,1)}, u32[]{:S(2)}, u32[]{:S(2)}) async-start(bf16[128,2,768]{2,1,0:T(2,128)(2,1)} %reshape.194), calls=%async_computation.2 | async-start | bytes 786432 | tf_op jit(solution)/shard_map/all_to_all | solution.py:91
  210.3 45.2 %all-gather.6.cloned.1.call-start = ((), (), s32[]{:S(2)}) async-start(), calls=%async_computation.5 | async-start | bytes 3538944 | tf_op jit(solution)/shard_map/all_gather | solution.py:123
  228.3 0.9 copy-start.4
  228.5 2.4 copy-start.13
  229.2 0.8 copy-start.7
  230.9 93.4 %all-gather.8.cloned.1.call-start = ((), (), s32[]{:S(2)}) async-start(), calls=%async_computation.6 | async-start | bytes 3170304 | tf_op jit(solution)/shard_map/all_gather | solution.py:143
  267.1 2.7 copy-start.1
  332.5 0.7 copy-start.6
  333.5 0.6 copy-start.10
  344.8 4.8 %copy-start.5 = (f32[128,768]{1,0:T(8,128)S(1)}, f32[128,768]{1,0:T(8,128)}, u32[]{:S(2)}) copy-start(f32[128,768]{1,0:T(8,128)} %copy-done.4) | copy-start | bytes 1179652
  344.8 4.8 %copy-start.8 = (bf16[768,768]{1,0:T(8,128)(2,1)S(1)}, bf16[768,768]{1,0:T(8,128)(2,1)}, u32[]{:S(2)}) copy-start(bf16[768,768]{1,0:T(8,128)(2,1)} %param.27) | copy-start | bytes 3538948
Sparse Core Ops, SparseCore 0:
  11.3 64.6 all-gather.3
  96.7 95.5 reduce-scatter.1
  231.0 24.3 all-gather.5
  258.4 65.8 all-gather.7
where the time goes:
time: 358 us; the launch traced here: 357 us
  waiting for transfers between devices  210 us (59%)
  local copies, waits for them, and re-layouts  56.9 us (16%)
  matrix products  36.7 us (10%)
  other arithmetic  24.2 us (7%)
  starting transfers between devices  16.2 us (5%)
  between operations  13.4 us (4%)
    reduce_scatter x1, waiting for transfers between devices, body(): lax.psum_scatter(jnp.dot(hidden, w_down, preferred_element_type=jnp.float...  68.9 us
    all_gather x1, waiting for transfers between devices, body(): shard_rows = lax.all_gather(normed, 'tile', axis=0, tiled=True)  64.7 us
    all_gather x1, waiting for transfers between devices, body(): lax.all_gather(select(keys_values, 2), ('tile', 'seq'), axis=0, tiled=True)  52.7 us
    dot_general x1, matrix products, body(): jnp.dot(hidden, w_down, preferred_element_type=jnp.float32)  14.6 us
    all_to_all x1, waiting for transfers between devices, body(): lax.all_to_all(meta_table.reshape(devices, capacity, 3), ('tile', 'seq'),...  9.2 us
    all_gather x1, waiting for transfers between devices, body(): segment_kv = lax.all_gather(keys_values, 'seq', axis=0, tiled=True)  8.69 us
    all_to_all x1, starting transfers between devices, body(): lax.all_to_all(meta_table.reshape(devices, capacity, 3), ('tile', 'seq'),...  8.32 us
    all_to_all x1, starting transfers between devices, body(): lax.all_to_all(payload.reshape(devices, capacity, hidden_width), ('tile',...  7.79 us
  transfers between devices with their start and end apart: 6, of which 6 were waited for; matrix products, arithmetic and copies ran while one was open for 13% of the time, Pallas kernels for 0%

commit v1 on v0

--- a/solution.py
+++ b/solution.py
@@ -140,7 +140,11 @@
         )
         return sampled_rows.reshape(resident_rows // SEGMENT_SPACING, stacked_rows * hidden_width)
 
-    far_kv = lax.all_gather(select(keys_values, 2), ("tile", "seq"), axis=0, tiled=True)
+    block = select(keys_values, 2)
+    devices_2 = lax.axis_size(("tile", "seq"))
+    blocks = jnp.stack([block for _ in range(devices_2)])
+    blocks = lax.all_to_all(blocks, ("tile", "seq"), split_axis=0, concat_axis=0)
+    far_kv = jnp.concatenate(blocks, axis=0)
     far_out, far_lse = attend(
         select(queries, 1).reshape(-1, HEAD_COUNT, HEAD_WIDTH),
         far_kv[:, :hidden_width].reshape(-1, HEAD_COUNT, HEAD_WIDTH),

time: 358 us -> 320 us (0.89)
  local copies, waits for them, and re-layouts: 56.9 us -> 38.6 us
  waiting for transfers between devices: 210 us -> 195 us
  matrix products: 36.7 us -> 29.5 us
  starting transfers between devices: 16.2 us -> 20.7 us
    all_gather x1 -> x0, waiting for transfers between devices: 52.7 us -> none  [body(): lax.all_gather(select(keys_values, 2), ('tile', 'seq'), axis=0, tiled=True)]
    all_to_all x0 -> x1, waiting for transfers between devices: none -> 46.8 us  [body(): lax.all_to_all(blocks, ('tile', 'seq'), split_axis=0, concat_axis=0)]
    all_gather x1, waiting for transfers between devices: 8.69 us -> 0.01 us  [body(): segment_kv = lax.all_gather(keys_values, 'seq', axis=0, tiled=True)]
    dot_general x2, matrix products: 6.91 us -> 1.98 us  [attend(): jnp.einsum('hqk,khd->qhd', weights.astype(jnp.bfloat16), values, preferre...]
    all_to_all x0 -> x1, starting transfers between devices: none -> 4.55 us  [body(): lax.all_to_all(blocks, ('tile', 'seq'), split_axis=0, concat_axis=0)]
    unnamed x29 -> x37, local copies, waits for them, and re-layouts: 6.38 us -> 2.53 us
  transfers between devices with their start and end apart: 6 -> 6, of which waited for: 6 -> 5; matrix products, arithmetic and copies ran while one was open for 13% -> 11% of each run, Pallas kernels for 0% -> 0%
where the time goes in v1:
time: 320 us; the launch traced here: 319 us
  waiting for transfers between devices  195 us (61%)
  local copies, waits for them, and re-layouts  38.6 us (12%)
  matrix products  29.5 us (9%)
  other arithmetic  21 us (7%)
  starting transfers between devices  20.7 us (6%)
  between operations  13.4 us (4%)
    reduce_scatter x1, waiting for transfers between devices, body(): lax.psum_scatter(jnp.dot(hidden, w_down, preferred_element_type=jnp.float...  68.9 us
    all_gather x1, waiting for transfers between devices, body(): shard_rows = lax.all_gather(normed, 'tile', axis=0, tiled=True)  64.7 us
    all_to_all x1, waiting for transfers between devices, body(): lax.all_to_all(blocks, ('tile', 'seq'), split_axis=0, concat_axis=0)  46.8 us
    dot_general x1, matrix products, body(): jnp.dot(hidden, w_down, preferred_element_type=jnp.float32)  14.6 us
    all_to_all x1, waiting for transfers between devices, body(): lax.all_to_all(meta_table.reshape(devices, capacity, 3), ('tile', 'seq'),...  9.2 us
    all_to_all x1, starting transfers between devices, body(): lax.all_to_all(meta_table.reshape(devices, capacity, 3), ('tile', 'seq'),...  8.32 us
    all_to_all x1, starting transfers between devices, body(): lax.all_to_all(payload.reshape(devices, capacity, hidden_width), ('tile',...  7.79 us
  transfers between devices with their start and end apart: 6, of which 5 were waited for; matrix products, arithmetic and copies ran while one was open for 11% of the time, Pallas kernels for 0%

profile of v1, /device:TPU:1, one launch (start us, length us, event | category | flops | bytes accessed | tf_op | source)
XLA Modules:
  0.0 318.6 jit_solution(17096413224237292461)
XLA Ops:
  6.5 1.3 convert_reduce_fusion
  7.8 1.2 fusion.31
  9.1 2.0 fusion.33
  11.2 64.7 %all-gather.3.cloned.1.call-done = bf16[2048,1536]{1,0:T(8,128)(2,1)} async-done(((bf16[128,1536]{1,0:T(8,128)(2,1)}), bf16[2048,1536]{1,0:T(8,128)(2,1)}) %all-gather.3.cloned.1.call-update) | async-done | bytes 6291472 | tf_op jit(solution)/shard_map/all_gather | solution.py:64
  75.9 6.1 %fusion.70 = f32[2048,256]{1,0:T(8,128)} fusion(bf16[2048,1536]{1,0:T(8,128)(2,1)} %all-gather.3.cloned.1.call-done, bf16[1536,256]{1,0:T(8,128)(2,1)} %param.16), kind=kOutput, calls=%fused_computation.112 | convolution fusion | flops 1610612736 | bytes 9175040 | tf_op jit(solution)/shard_map/dot_general | solution.py:65
  82.0 14.6 %fusion.7 = f32[2048,1536]{1,0:T(8,128)} fusion(bf16[256,1536]{1,0:T(8,128)(2,1)} %param.18, bf16[2048,1536]{1,0:T(8,128)(2,1)} %all-gather.3.cloned.1.call-done, bf16[1536,256]{1,0:T(8,128)(2,1)} %param.17, f32[2048,256]{1,0:T(8,128)} %fusion.70), kind=kOutput, calls=%fused_computation.14 | convolution fusion | flops 3224371200 | bytes 22544384 | tf_op jit(solution)/shard_map/dot_general | solution.py:69
  96.6 0.8 slice_bitcast_fusion.1
  97.4 1.2 pad_add_fusion
  98.6 1.4 copy.64
  100.0 0.7 and_select_fusion.1
  100.7 0.2 convert_reduce_fusion.1
  100.9 1.2 compare_select_fusion.4
  102.0 1.8 scatter_custom_fusion
  103.8 8.3 %all-to-all-start = ((s32[128,2,3]{2,1,0:T(2,128)}), s32[128,2,3]{2,1,0:T(2,128)}, u32[]{:S(2)}, u32[]{:S(2)}) async-start(s32[128,2,3]{2,1,0:T(2,128)} %bitcast.78), calls=%async_computation | async-start | bytes 262144 | tf_op jit(solution)/shard_map/all_to_all | solution.py:98
  112.2 0.6 negate_power_fusion
  112.8 9.2 %all-to-all-done = s32[128,2,3]{2,1,0:T(2,128)} async-done(((s32[128,2,3]{2,1,0:T(2,128)}), s32[128,2,3]{2,1,0:T(2,128)}, u32[]{:S(2)}, u32[]{:S(2)}) %all-to-all-start) | async-done | bytes 3104 | tf_op jit(solution)/shard_map/all_to_all | solution.py:98
  122.0 1.5 copy.82
  123.5 68.9 %reduce-scatter.2.cloned.1.call-done = f32[128,1536]{1,0:T(8,128)} async-done(((f32[2048,1536]{1,0:T(8,128)}), f32[128,1536]{1,0:T(8,128)}) %reduce-scatter.2.cloned.1.call-update) | async-done | bytes 786448 | tf_op jit(solution)/shard_map/reduce_scatter | solution.py:68
  192.4 1.5 fusion.39
  193.9 1.5 multiply_reduce_fusion.1
  195.4 2.9 convolution_convert_fusion.1
  198.3 2.3 scatter_custom_fusion.1
  200.6 1.9 reshape.196
  202.5 7.8 %all-to-all-start.1 = ((bf16[128,2,768]{2,1,0:T(2,128)(2,1)}), bf16[128,2,768]{2,1,0:T(2,128)(2,1)}, u32[]{:S(2)}, u32[]{:S(2)}) async-start(bf16[128,2,768]{2,1,0:T(2,128)(2,1)} %reshape.196), calls=%async_computation.2 | async-start | bytes 786432 | tf_op jit(solution)/shard_map/all_to_all | solution.py:91
  210.3 0.6 compare_select_fusion
  211.0 2.2 scatter_custom_fusion.3
  213.2 1.1 fusion.52
  214.3 2.5 multiply_sine_fusion.1
  216.7 5.6 %all-to-all-done.1 = bf16[128,2,768]{2,1,0:T(2,128)(2,1)} async-done(((bf16[128,2,768]{2,1,0:T(2,128)(2,1)}), bf16[128,2,768]{2,1,0:T(2,128)(2,1)}, u32[]{:S(2)}, u32[]{:S(2)}) %all-to-all-start.1) | async-done | bytes 393248 | tf_op jit(solution)/shard_map/all_to_all | solution.py:91
  222.3 1.9 reshape.226
  224.2 2.7 scatter_custom_fusion.2
  226.9 1.4 fusion.66
  228.3 0.2 multiply_reduce_fusion.2
  228.6 0.7 convolution_convert_fusion
  229.3 0.8 copy-done.7
  230.1 0.8 slice.54
  230.9 1.8 reshape.201
  232.7 0.4 select_reduce_fusion
  233.1 0.1 stack_reshape.2
  233.2 1.9 stack.11
  235.1 4.6 %all-to-all-start.2 = ((bf16[128,8,1536]{2,1,0:T(8,128)(2,1)}), bf16[128,8,1536]{2,1,0:T(8,128)(2,1)S(1)}, u32[]{:S(2)}, u32[]{:S(2)}) async-start(bf16[128,8,1536]{2,1,0:T(8,128)(2,1)} %stack.11), calls=%async_computation.3 | async-start | bytes 6291456 | tf_op jit(solution)/shard_map/all_to_all | solution.py:146
  239.7 0.1 copy.69
  239.8 0.7 broadcast_in_dim.119
  240.5 0.9 slice.53
  241.4 0.8 copy.70
  242.2 1.1 reshape.200
  243.4 1.9 select_reduce_fusion.1
  245.3 46.8 %all-to-all-done.2 = bf16[128,8,1536]{2,1,0:T(8,128)(2,1)S(1)} async-done(((bf16[128,8,1536]{2,1,0:T(8,128)(2,1)}), bf16[128,8,1536]{2,1,0:T(8,128)(2,1)S(1)}, u32[]{:S(2)}, u32[]{:S(2)}) %all-to-all-start.2) | async-done | bytes 3145760 | tf_op jit(solution)/shard_map/all_to_all | solution.py:146
  292.0 1.9 fusion.67
  293.9 1.8 copy.72
  295.8 1.2 fusion.69
  296.9 0.2 fusion.38
  297.2 0.1 sub.77
  297.2 0.7 sub.78
  297.9 0.7 copy.75
  298.7 0.6 fusion.15
  299.3 1.0 copy.78
  300.4 3.2 %fusion.68 = (bf16[1024,768]{1,0:T(8,128)(2,1)}, bf16[1024,768]{1,0:T(8,128)(2,1)S(1)}) fusion(bf16[1024,1536]{1,0:T(8,128)(2,1)} %all-gather.5.cloned.1.call-done), kind=kLoop, calls=%fused_computation.110 | loop fusion | bytes 6291456 | tf_op jit(solution)/shard_map/slice | solution.py:126
  303.6 1.7 copy.71
  305.3 1.7 copy.74
  307.0 1.1 multiply_reduce_fusion
  308.1 1.3 fusion.1
  309.6 1.4 fusion.26
  311.0 1.0 fusion.14
  (53 shorter events, 0.5 us)
Async XLA Ops:
  6.5 222.0 %copy-start = (bf16[768,2304]{1,0:T(8,128)(2,1)S(1)}, bf16[768,2304]{1,0:T(8,128)(2,1)}, u32[]{:S(2)}) copy-start(bf16[768,2304]{1,0:T(8,128)(2,1)} %param.25) | copy-start | bytes 10616836
  6.5 69.4 %all-gather.3.cloned.1.call-start = ((), (), s32[]{:S(2)}) async-start(), calls=%async_computation.4 | async-start | bytes 6684672 | tf_op jit(solution)/shard_map/all_gather | solution.py:64
  11.1 181.2 %reduce-scatter.2.cloned.1.call-start = ((), (), s32[]{:S(2)}) async-start(), calls=%async_computation.5 | async-start | bytes 13369344 | tf_op jit(solution)/shard_map/reduce_scatter | solution.py:68
  96.6 95.8 %copy-start.12 = (f32[1536]{0:T(1024)S(1)}, f32[1536]{0:T(1024)}, u32[]{:S(2)}) copy-start(f32[1536]{0:T(1024)} %param.19) | copy-start | bytes 18436
  96.6 98.8 %copy-start.14 = (f32[1536]{0:T(1024)S(1)}, f32[1536]{0:T(1024)}, u32[]{:S(2)}) copy-start(f32[1536]{0:T(1024)} %param.20) | copy-start | bytes 18436
  103.8 18.1 %all-to-all-start = ((s32[128,2,3]{2,1,0:T(2,128)}), s32[128,2,3]{2,1,0:T(2,128)}, u32[]{:S(2)}, u32[]{:S(2)}) async-start(s32[128,2,3]{2,1,0:T(2,128)} %bitcast.78), calls=%async_computation | async-start | bytes 262144 | tf_op jit(solution)/shard_map/all_to_all | solution.py:98
  192.4 3.0 copy-start.2
  192.4 3.0 copy-start.3
  200.6 28.0 %copy-start.16 = (f32[768]{0:T(1024)S(1)}, f32[768]{0:T(1024)}, u32[]{:S(2)}) copy-start(f32[768]{0:T(1024)} %param.24) | copy-start | bytes 9220
  202.5 19.8 %all-to-all-start.1 = ((bf16[128,2,768]{2,1,0:T(2,128)(2,1)}), bf16[128,2,768]{2,1,0:T(2,128)(2,1)}, u32[]{:S(2)}, u32[]{:S(2)}) async-start(bf16[128,2,768]{2,1,0:T(2,128)(2,1)} %reshape.196), calls=%async_computation.2 | async-start | bytes 786432 | tf_op jit(solution)/shard_map/all_to_all | solution.py:91
  210.3 90.1 %all-gather.5.cloned.1.call-start = ((), (), s32[]{:S(2)}) async-start(), calls=%async_computation.6 | async-start | bytes 3538944 | tf_op jit(solution)/shard_map/all_gather | solution.py:123
  228.3 0.9 copy-start.5
  228.5 2.3 copy-start.17
  229.2 0.8 copy-start.7
  235.1 56.9 %all-to-all-start.2 = ((bf16[128,8,1536]{2,1,0:T(8,128)(2,1)}), bf16[128,8,1536]{2,1,0:T(8,128)(2,1)S(1)}, u32[]{:S(2)}, u32[]{:S(2)}) async-start(bf16[128,8,1536]{2,1,0:T(8,128)(2,1)} %stack.11), calls=%async_computation.3 | async-start | bytes 6291456 | tf_op jit(solution)/shard_map/all_to_all | solution.py:146
  293.9 4.0 %copy-start.4 = (bf16[1024,768]{1,0:T(8,128)(2,1)S(1)}, bf16[1024,768]{1,0:T(8,128)(2,1)}, u32[]{:S(2)}) copy-start(bf16[1024,768]{1,0:T(8,128)(2,1)} %get-tuple-element.12) | copy-start | bytes 4718596
  305.3 1.7 copy-start.10
  308.1 1.3 copy-start.13
  308.1 1.3 copy-start.15
  308.1 1.4 copy-start.8
  308.1 1.5 copy-start.11
  309.6 1.4 copy-start.6
  309.6 1.4 copy-start.9
  309.6 2.5 copy-start.1
Sparse Core Ops, SparseCore 0:
  11.3 64.6 all-gather.2
  96.7 95.5 reduce-scatter.1
  231.0 45.6 all-gather.4
